TPU v7x, 256 devices: a whole 4x4x8 slice. The times are simulated.
256 devices in a mesh: rows: 8 (over x, core), vocab: 32 (over y, z).
Axes of the slice: x: 4, y: 4, z: 8, core: 2. Of those that a mesh axis runs over, the one named last changes fastest.
Arguments:
- hidden: bfloat16 [1536, 8192], P(None, 'rows'), may hold values from -32 to 32
- table: bfloat16 [65536, 8192], P('vocab', 'rows'), may hold values from -0.5 to 0.5
- subset_ids: int32 [32768], P('vocab'), may hold values from 0 to 65535, as said below
- targets: bfloat16 [1536, 32768], P('rows', 'vocab'), may hold values from 0 to 1, as said below
Outputs:
- draft_logits: bfloat16 [1536, 32768], P('rows', 'vocab')
- hidden_grad: bfloat16 [1536, 8192], P('vocab', 'rows')
- table_grad: bfloat16 [65536, 8192], P('vocab', 'rows')
Inputs may be any that keep to these rules, and one draw needn't show every extreme that they name: `subset_ids`: all ids differ. Table shard o holds ids o * 2048 to (o + 1) * 2048 - 1. Among the 1024 ids of one vocab shard, a quarter of the table shards hold 64 each, a quarter 64 / 2 each and the other half 64 / 4 each; one table shard holds 64 ids of every vocab shard. `targets`: Positive.
All inputs are finite; a program needn't handle non-finite values.
Results may differ from a plain program's by a relative error of at most 0.0049.
Values may be sent and summed in bfloat16 or wider, within the bound.
No kernel may reach another device: no remote copies, remote signals or barrier semaphores. Data moves between devices by JAX's collectives and lax.ppermute only.
A program may use at most 128 MiB of HBM per device.

v0:
```python
import jax
import jax.numpy as jnp
from jax import lax
from jax.sharding import PartitionSpec as P

LOSS_SCALE = 32.0


def against_rows(left, head_rows):
    return lax.dot_general(
        left, head_rows, (((1,), (1,)), ((), ())), preferred_element_type=jnp.float32
    )


def on_device(hidden, table, subset_ids, targets):
    vocab_count = lax.axis_size("vocab")
    sub_dev = subset_ids.shape[0]
    capacity = 2 * sub_dev // vocab_count
    owner_rows = table.shape[0]
    col_width = table.shape[1]
    owner_of = subset_ids // owner_rows
    local_row = subset_ids % owner_rows
    onehot = (owner_of[:, None] == jnp.arange(vocab_count)[None, :]).astype(jnp.int32)
    before = jnp.cumsum(onehot, axis=0) - onehot
    slot_rank = jnp.sum(before * onehot, axis=1)
    slot_index = owner_of * capacity + slot_rank
    request = jnp.zeros((vocab_count * capacity,), jnp.int32).at[slot_index].set(local_row)
    request = request.reshape(vocab_count, capacity)
    asked_rows = lax.all_to_all(request, "vocab", split_axis=0, concat_axis=0, tiled=True)
    picked = table[asked_rows]
    fetched = lax.all_to_all(picked, "vocab", split_axis=0, concat_axis=0, tiled=True)
    head_rows = fetched.reshape(vocab_count * capacity, col_width)[slot_index]
    positions = hidden.shape[0]
    pos_dev = positions // lax.axis_size("rows")
    partial_logits = against_rows(hidden, head_rows)
    summed = lax.psum(partial_logits, "rows")
    logits = lax.dynamic_slice_in_dim(summed, lax.axis_index("rows") * pos_dev, pos_dev, 0)
    target = targets.astype(jnp.float32)
    local_mass = jnp.sum(target, axis=1)
    local_peak = jnp.max(logits, axis=1)
    row_peak = lax.pmax(local_peak, "vocab")
    local_total = jnp.sum(jnp.exp(logits - row_peak[:, None]), axis=1)
    row_total, row_mass = lax.psum((local_total, local_mass), "vocab")
    softmax_probs = jnp.exp(logits - row_peak[:, None]) / row_total[:, None]
    logit_grad = (LOSS_SCALE * (softmax_probs * row_mass[:, None] - target)).astype(jnp.bfloat16)
    grad_all = lax.all_gather(logit_grad, "rows", axis=0, tiled=True)
    row_grad = lax.dot_general(
        grad_all, hidden, (((0,), (0,)), ((), ())), preferred_element_type=jnp.float32
    ).astype(jnp.bfloat16)
    hidden_grad = lax.psum_scatter(
        jnp.dot(grad_all, head_rows, preferred_element_type=jnp.float32),
        "vocab",
        scatter_dimension=0,
        tiled=True,
    ).astype(jnp.bfloat16)
    outgoing = (
        jnp.zeros((vocab_count * capacity, col_width), jnp.bfloat16).at[slot_index].set(row_grad)
    )
    outgoing = outgoing.reshape(vocab_count, capacity, col_width)
    returned = lax.all_to_all(outgoing, "vocab", split_axis=0, concat_axis=0, tiled=True)
    table_grad = (
        jnp.zeros(table.shape, jnp.bfloat16)
        .at[asked_rows.reshape(-1)]
        .add(returned.reshape(-1, col_width))
    )
    return (logits.astype(jnp.bfloat16), hidden_grad, table_grad)


def solution(mesh):
    return jax.shard_map(
        on_device,
        mesh=mesh,
        in_specs=(P(None, "rows"), P("vocab", "rows"), P("vocab"), P("rows", "vocab")),
        out_specs=(P("rows", "vocab"), P("vocab", "rows"), P("vocab", "rows")),
        check_vma=False,
    )
```

profile of v0, /device:TPU:2, one launch (start us, length us, event | category | flops | bytes accessed | tf_op | source)
XLA Modules:
  0.0 716.7 jit_solution(17530156705995859926)
XLA Ops:
  7.2 0.0 copy-start
  7.2 0.0 all-reduce.3.cloned.1.call-start
  7.2 0.8 add_select_fusion
  8.1 9.0 %reduce-window.6 = s32[32,8,128]{2,1,0:T(8,128)S(1)} reduce-window(s32[32,8,128]{2,1,0:T(8,128)S(1)} %fusion.11, s32[]{:T(128)} %constant.23.clone.1), window={size=1x1x128 pad=0_0x0_0x127_0}, to_apply=%region_0.1 | reduce-window | flops 4161536 | bytes 262148 | tf_op jit(solution)/shard_map/reduce-window
  17.1 0.1 slice.12
  17.2 0.1 copy.18
  17.4 0.1 copy.19
  17.4 0.1 broadcast_add_fusion
  17.6 0.0 copy-start.2
  17.6 0.6 copy-done.2
  18.2 4.3 scatter_custom_fusion
  22.5 0.1 all_to_all.14
  22.6 21.1 %all_to_all.22 = s32[32,1,64]{2,1,0:T(1,128)S(1)} all-to-all(s32[32,1,64]{2,1,0:T(1,128)S(1)} %all_to_all.14), channel_id=1, replica_groups=mesh['rows'=8,'vocab'=32] {'vocab'}, dimensions={0} | all-to-all | bytes 16384 | tf_op jit(solution)/shard_map/all_to_all | solution.py:29
  43.7 0.1 reshape.105
  43.8 13.7 %gather_fusion = bf16[2048,1024]{1,0:T(8,128)(2,1)} fusion(bf16[2048,1024]{1,0:T(8,128)(2,1)} %param.5, s32[2048]{0:T(1024)S(1)} %broadcast_clamp_fusion), kind=kCustom, calls=%fused_computation | custom fusion | bytes 8396800 | tf_op jit(solution)/shard_map/gather | solution.py:30
  57.4 99.8 %all_to_all.23 = bf16[32,64,1024]{2,1,0:T(8,128)(2,1)} all-to-all(bf16[32,64,1024]{2,1,0:T(8,128)(2,1)} %bitcast.36), channel_id=1, replica_groups=mesh['rows'=8,'vocab'=32] {'vocab'}, dimensions={0} | all-to-all | bytes 8388608 | tf_op jit(solution)/shard_map/all_to_all | solution.py:31
  157.2 8.7 %gather_fusion.1 = bf16[1024,1024]{1,0:T(8,128)(2,1)} fusion(bf16[2048,1024]{1,0:T(8,128)(2,1)} %bitcast.35, s32[1024]{0:T(1024)S(1)} %get-tuple-element.14), kind=kCustom, calls=%fused_computation.1 | custom fusion | bytes 4198400 | tf_op jit(solution)/shard_map/gather | solution.py:32
  166.0 0.0 copy-done
  166.0 6.9 convolution_bitcast_fusion
  172.8 0.0 copy-start.1
  172.8 0.0 all-reduce.3.cloned.1.call-update
  172.9 0.0 all-gather.2.cloned.1.call-start
  172.9 0.9 copy-done.1
  173.8 0.7 convert_reduce_fusion
  174.5 81.9 %all-reduce.3.cloned.1.call-done = f32[1536,1024]{1,0:T(8,128)} async-done(((f32[1536,1024]{1,0:T(8,128)}), f32[1536,1024]{1,0:T(8,128)}) %all-reduce.3.cloned.1.call-update) | async-done | bytes 6291472 | tf_op jit(solution)/shard_map/psum | solution.py:36
  256.4 1.8 dynamic-slice_reduce_fusion
  258.3 75.9 %pmax.7 = f32[192]{0:T(256)} all-reduce(f32[192]{0:T(256)} %dynamic-slice_reduce_fusion), channel_id=1, replica_groups=mesh['rows'=8,'vocab'=32] {'vocab'}, use_global_device_ids=true, to_apply=%region_6.7 | all-reduce | flops 192 | bytes 1536 | tf_op jit(solution)/shard_map/pmax | solution.py:41
  334.2 2.0 fusion.7
  336.1 70.3 %all-reduce = (f32[192]{0:T(256)}, f32[192]{0:T(256)}) all-reduce(f32[192]{0:T(256)} %convert_reduce_fusion, f32[192]{0:T(256)} %fusion.7), channel_id=1, replica_groups=mesh['rows'=8,'vocab'=32] {'vocab'}, use_global_device_ids=true, to_apply=%region_10.11 | all-reduce | flops 384 | bytes 3072 | tf_op jit(solution)/shard_map/psum | solution.py:43
  406.5 2.2 fusion.6
  408.7 0.0 all-gather.2.cloned.1.call-update
  408.7 0.2 reduce-scatter.2.cloned.1.call-start
  408.9 24.3 %all-gather.2.cloned.1.call-done = bf16[1536,1024]{1,0:T(8,128)(2,1)} async-done(((bf16[192,1024]{1,0:T(8,128)(2,1)}), bf16[1536,1024]{1,0:T(8,128)(2,1)}) %all-gather.2.cloned.1.call-update) | async-done | bytes 3145744 | tf_op jit(solution)/shard_map/all_gather | solution.py:46
  433.2 8.6 %fusion.16 = f32[1536,1024]{1,0:T(8,128)} fusion(bf16[1536,1024]{1,0:T(8,128)(2,1)} %all-gather.2.cloned.1.call-done, bf16[1024,1024]{1,0:T(8,128)(2,1)} %gather_fusion.1), kind=kOutput, calls=%fused_computation.42 | convolution fusion | flops 3221225472 | bytes 11534336 | tf_op jit(solution)/shard_map/dot_general | solution.py:51
  441.9 0.0 reduce-scatter.2.cloned.1.call-update
  441.9 6.9 fusion.17
  448.8 8.9 %scatter_custom_fusion.1 = bf16[2048,1024]{1,0:T(8,128)(2,1)} fusion(s32[1024]{0:T(1024)} %copy-done.2, f32[1024,1024]{1,0:T(8,128)} %fusion.17, bf16[]{:T(256)} %constant.58.clone.1), kind=kCustom, calls=%fused_computation.6 | custom fusion | flops 1048576 | bytes 8389120 | tf_op jit(solution)/shard_map/scatter | solution.py:57
  457.7 10.2 %all-to-all-start.2 = ((bf16[32,64,1024]{2,1,0:T(8,128)(2,1)}), bf16[32,64,1024]{2,1,0:T(8,128)(2,1)}, u32[]{:S(2)}, u32[]{:S(2)}) async-start(bf16[32,64,1024]{2,1,0:T(8,128)(2,1)} %bitcast.37), calls=%async_computation.3 | async-start | bytes 8388608 | tf_op jit(solution)/shard_map/all_to_all | solution.py:60
  467.9 0.5 broadcast.96
  468.4 0.7 reduce.3
  469.1 0.1 reshape.100
  469.2 2.0 dynamic-slice_convert_fusion
  471.2 115.1 %all-to-all-done.2 = bf16[32,64,1024]{2,1,0:T(8,128)(2,1)} async-done(((bf16[32,64,1024]{2,1,0:T(8,128)(2,1)}), bf16[32,64,1024]{2,1,0:T(8,128)(2,1)}, u32[]{:S(2)}, u32[]{:S(2)}) %all-to-all-start.2) | async-done | bytes 4194336 | tf_op jit(solution)/shard_map/all_to_all | solution.py:60
  586.2 21.0 %scatter_custom_fusion.2 = bf16[2048,1024]{1,0:T(8,128)(2,1)} fusion(s32[2048]{0:T(1024)S(1)} %bitcast.42, bf16[2048,1024]{1,0:T(8,128)(2,1)} %bitcast.9, bf16[]{:T(256)} %constant.58.clone.1), kind=kCustom, calls=%fused_computation.8 | custom fusion | flops 2097152 | bytes 4194816 | tf_op jit(solution)/shard_map/scatter-add | solution.py:64
  607.2 101.4 %reduce-scatter.2.cloned.1.call-done = f32[48,1024]{1,0:T(8,128)} async-done(((f32[1536,1024]{1,0:T(8,128)}), f32[48,1024]{1,0:T(8,128)}) %reduce-scatter.2.cloned.1.call-update) | async-done | bytes 196624 | tf_op jit(solution)/shard_map/reduce_scatter | solution.py:50
  708.6 1.6 convert_element_type.27
  (8 shorter events, 0.1 us)
Async XLA Ops:
  7.2 158.8 %copy-start = (bf16[1536,1024]{1,0:T(8,128)(2,1)S(1)}, bf16[1536,1024]{1,0:T(8,128)(2,1)}, u32[]{:S(2)}) copy-start(bf16[1536,1024]{1,0:T(8,128)(2,1)} %param.4) | copy-start | bytes 9437188
  7.2 249.3 %all-reduce.3.cloned.1.call-start = ((), (), s32[]{:S(2)}) async-start(), calls=%async_computation.4 | async-start | bytes 12582912 | tf_op jit(solution)/shard_map/psum | solution.py:36
  17.6 0.6 copy-start.2
  172.8 1.0 copy-start.1
  172.9 260.4 %all-gather.2.cloned.1.call-start = ((), (), s32[]{:S(2)}) async-start(), calls=%async_computation.5 | async-start | bytes 3538944 | tf_op jit(solution)/shard_map/all_gather | solution.py:46
  408.7 299.9 %reduce-scatter.2.cloned.1.call-start = ((), (), s32[]{:S(2)}) async-start(), calls=%async_computation.6 | async-start | bytes 6488064 | tf_op jit(solution)/shard_map/reduce_scatter | solution.py:50
  457.7 128.5 %all-to-all-start.2 = ((bf16[32,64,1024]{2,1,0:T(8,128)(2,1)}), bf16[32,64,1024]{2,1,0:T(8,128)(2,1)}, u32[]{:S(2)}, u32[]{:S(2)}) async-start(bf16[32,64,1024]{2,1,0:T(8,128)(2,1)} %bitcast.37), calls=%async_computation.3 | async-start | bytes 8388608 | tf_op jit(solution)/shard_map/all_to_all | solution.py:60
Sparse Core Ops, SparseCore 0:
  173.0 83.4 all-reduce.2
  408.8 24.3 all-gather.1
  442.0 266.5 reduce-scatter.1
where the time goes:
time: 717 us
  waiting for transfers between devices  323 us (45%)
  blocking collectives  267 us (37%)
  other arithmetic  49 us (7%)
  local copies, waits for them, and re-layouts  31.2 us (4%)
  matrix products  22.4 us (3%)
  between operations  13.9 us (2%)
  starting transfers between devices  10.5 us (1%)
    all_to_all x1, waiting for transfers between devices, on_device(): lax.all_to_all(outgoing, 'vocab', split_axis=0, concat_axis=0, tiled=True)  115 us
    reduce_scatter x1, waiting for transfers between devices, on_device(): lax.psum_scatter(jnp.dot(grad_all, head_rows, preferred_element_type=jnp....  101 us
    all_to_all x1, blocking collectives, on_device(): lax.all_to_all(picked, 'vocab', split_axis=0, concat_axis=0, tiled=True)  99.8 us
    psum x1, waiting for transfers between devices, on_device(): summed = lax.psum(partial_logits, 'rows')  81.9 us
    pmax x1, blocking collectives, on_device(): row_peak = lax.pmax(local_peak, 'vocab')  75.9 us
    psum x1, blocking collectives, on_device(): row_total, row_mass = lax.psum((local_total, local_mass), 'vocab')  70.3 us
    all_gather x1, waiting for transfers between devices, on_device(): grad_all = lax.all_gather(logit_grad, 'rows', axis=0, tiled=True)  24.3 us
    all_to_all x1, blocking collectives, on_device(): lax.all_to_all(request, 'vocab', split_axis=0, concat_axis=0, tiled=True)  21.1 us
  transfers between devices with their start and end apart: 4, of which 4 were waited for; matrix products, arithmetic and copies ran while one was open for 6% of the time, Pallas kernels for 0%

commit v1 on v0

v1 whole, which is shorter than its diff:
```python
import jax
import jax.numpy as jnp
from jax import lax
from jax.sharding import Mesh, PartitionSpec as P

LOSS_SCALE = 32.0
LOW = 64
FAR = -3.0e38
ROWS = ("x", "core")
VOCAB = ("y", "z")
f32, bf16, i32, i16 = jnp.float32, jnp.bfloat16, jnp.int32, jnp.int16


def shift(axis, by):
    n = lax.axis_size(axis)
    return [(i, (i + by) % n) for i in range(n)]


def matmul(a, b, ca, cb, dtype=f32):
    return lax.dot_general(a, b, (((ca,), (cb,)), ((), ())), preferred_element_type=dtype)


def at(blocks, index):
    return lax.dynamic_index_in_dim(blocks, index, 0, keepdims=False)


def encode(part):
    top = jnp.maximum(jnp.max(jnp.abs(part), axis=-1, keepdims=True), 1e-30)
    return jnp.round(part * (32767.0 / top)).astype(i16), top * (1.0 / 32767.0)


def slots_of(subset_ids, owner_rows, vocab_count, capacity):
    count = subset_ids.shape[0]
    owner_of = subset_ids // owner_rows
    onehot = (owner_of[:, None] == jnp.arange(vocab_count)[None, :]).astype(bf16)
    earlier = (jnp.arange(count)[:, None] > jnp.arange(count)[None, :]).astype(bf16)
    before = matmul(earlier, onehot, 1, 0)
    rank = jnp.sum(before * onehot.astype(f32), axis=1).astype(i32)
    return owner_of * capacity + rank, subset_ids % owner_rows


def on_device(hidden, table, subset_ids, targets):
    nx, nc, ny, nz = (lax.axis_size(a) for a in ("x", "core", "y", "z"))
    x, core, y, z = (lax.axis_index(a) for a in ("x", "core", "y", "z"))
    vocab_count = ny * nz
    positions, width = hidden.shape
    owner_rows = table.shape[0]
    sub_dev = subset_ids.shape[0]
    pos_dev = targets.shape[0]
    capacity = 2 * sub_dev // vocab_count
    slots = vocab_count * capacity

    own_hidden = hidden.reshape(nx, nc, pos_dev, width)
    swap = [(0, 1), (1, 0)]
    table_far = lax.ppermute(table, "core", swap)
    mine = lax.dynamic_index_in_dim(own_hidden, core, 1, keepdims=False)
    hidden_far = lax.ppermute(
        lax.dynamic_index_in_dim(own_hidden, 1 - core, 1, keepdims=False), "core", swap
    )

    slot_index, local_row = slots_of(subset_ids, owner_rows, vocab_count, capacity)
    to_slot = (jnp.arange(slots)[:, None] == slot_index[None, :]).astype(bf16)
    side = jnp.stack([local_row // LOW, local_row % LOW, jnp.ones_like(local_row)]).astype(bf16)
    pad = (-(pos_dev + side.shape[0])) % 128
    sent = jnp.concatenate([targets, side, jnp.zeros((pad, sub_dev), bf16)], axis=0)
    payload = matmul(to_slot, sent, 1, 1, bf16)
    got = lax.all_to_all(
        payload.reshape(vocab_count, capacity, -1), VOCAB, split_axis=0, concat_axis=0, tiled=True
    ).reshape(slots, -1)
    info = got[:, pos_dev : pos_dev + 3].astype(i32)
    row_of = jnp.where(info[:, 2] > 0, info[:, 0] * LOW + info[:, 1], -1)
    to_row = (row_of[:, None] == jnp.arange(owner_rows)[None, :]).astype(bf16)
    landed = matmul(got, to_row, 0, 0)
    target = landed[:pos_dev]
    chosen = landed[pos_dev + 2 : pos_dev + 3] > 0.5

    total = None
    arrived = []
    for k in (2, 1, 3, 0):
        to = (x + k) % nx
        part = matmul(at(mine, to), table, 1, 1) + matmul(at(hidden_far, to), table_far, 1, 1)
        if k == 0:
            total = part
            continue
        code, step = encode(part)
        arrived.append(
            (lax.ppermute(code, "x", shift("x", k)), lax.ppermute(step, "x", shift("x", k)))
        )
    logits = total
    for code, step in arrived:
        logits = logits + code.astype(f32) * step

    peak = jnp.max(jnp.where(chosen, logits, FAR), axis=1)
    part_total = jnp.sum(jnp.where(chosen, jnp.exp(logits - peak[:, None]), 0.0), axis=1)
    mass = jnp.sum(target, axis=1)
    stats = jnp.stack([peak, part_total, mass])
    stats = jnp.broadcast_to(stats[None], (vocab_count,) + stats.shape)
    stats = lax.all_to_all(stats, VOCAB, split_axis=0, concat_axis=0, tiled=True)
    row_peak = jnp.max(stats[:, 0], axis=0)
    row_total = jnp.sum(stats[:, 1] * jnp.exp(stats[:, 0] - row_peak[None, :]), axis=0)
    row_mass = jnp.sum(stats[:, 2], axis=0)
    probs = jnp.exp(logits - row_peak[:, None]) / row_total[:, None]
    grad = jnp.where(chosen, LOSS_SCALE * (probs * row_mass[:, None] - target), 0.0).astype(bf16)

    blocks = [grad] + [lax.ppermute(grad, "x", shift("x", -j)) for j in range(1, nx)]
    own = jnp.stack(blocks)
    other = lax.ppermute(own, "core", swap)
    first = jnp.where(core == 0, own, other)
    second = jnp.where(core == 0, other, own)
    grad_all = jnp.stack([first, second], axis=1)
    turned = jnp.stack([at(own_hidden, (x + j) % nx) for j in range(nx)])
    flat = grad_all.reshape(positions, owner_rows)
    table_grad = matmul(flat, turned.reshape(positions, width), 0, 0).astype(bf16)

    hidden_part = matmul(flat, table, 1, 0).reshape(nx, nc * pos_dev, width)
    mine_y = at(hidden_part, (y - x) % nx)
    for k in (2, 1, 3):
        code, step = encode(at(hidden_part, (y + k - x) % nx))
        code, step = (lax.ppermute(a, "y", shift("y", k)) for a in (code, step))
        mine_y = mine_y + code.astype(f32) * step
    out_pos = positions // vocab_count
    code, step = encode(mine_y.reshape(nz, out_pos, width))
    code, step = (
        lax.all_to_all(a, "z", split_axis=0, concat_axis=0, tiled=True) for a in (code, step)
    )
    hidden_grad = jnp.sum(code.astype(f32) * step, axis=0).astype(bf16)

    out = matmul(to_row, logits.astype(bf16), 1, 1, bf16)
    out = lax.all_to_all(
        out.reshape(vocab_count, capacity, pos_dev), VOCAB, split_axis=0, concat_axis=0, tiled=True
    ).reshape(slots, pos_dev)
    draft = matmul(out, to_slot, 0, 0, bf16)
    return draft, hidden_grad, table_grad


def solution(mesh):
    fine = Mesh(mesh.devices.reshape(4, 2, 4, 8), ROWS + VOCAB)
    return jax.shard_map(
        on_device,
        mesh=fine,
        in_specs=(P(None, ROWS), P(VOCAB, ROWS), P(VOCAB), P(ROWS, VOCAB)),
        out_specs=(P(ROWS, VOCAB), P(VOCAB, ROWS), P(VOCAB, ROWS)),
        check_vma=False,
    )
```

time: 717 us -> 288 us (0.40)
  blocking collectives: 267 us -> 18.5 us
  waiting for transfers between devices: 323 us -> 109 us
  starting transfers between devices: 10.5 us -> 55.9 us
  matrix products: 22.4 us -> 66.2 us
  other arithmetic: 49 us -> 18.4 us
  local copies, waits for them, and re-layouts: 31.2 us -> 14.4 us
  between operations: 13.9 us -> 1.57 us
    all_to_all x2 -> x1, blocking collectives: 121 us -> 18.5 us  [on_device(): lax.all_to_all(stats, VOCAB, split_axis=0, concat_axis=0, tiled=True)]
    reduce_scatter x1 -> x0, waiting for transfers between devices: 101 us -> none  [on_device(): lax.psum_scatter(jnp.dot(grad_all, head_rows, preferred_element_type=jnp....]
    all_to_all x1 -> x4, waiting for transfers between devices: 115 us -> 29.5 us  [the longest x2 17.8 us: on_device(): lax.all_to_all(a, 'z', split_axis=0, concat_axis=0, tiled=True)]
    psum x1 -> x0, waiting for transfers between devices: 81.9 us -> none  [on_device(): summed = lax.psum(partial_logits, 'rows')]
    ppermute x0 -> x18, waiting for transfers between devices: none -> 79.3 us  [the longest x6 30.9 us: on_device(): code, step = (lax.ppermute(a, 'y', shift('y', k)) for a in (code, step))]
    pmax x1 -> x0, blocking collectives: 75.9 us -> none  [on_device(): row_peak = lax.pmax(local_peak, 'vocab')]
    psum x1 -> x0, blocking collectives: 70.3 us -> none  [on_device(): row_total, row_mass = lax.psum((local_total, local_mass), 'vocab')]
    dot_general x3 -> x15, matrix products: 22.4 us -> 66.2 us  [matmul(): lax.dot_general(a, b, (((ca,), (cb,)), ((), ())), preferred_element_type=...]
  transfers between devices with their start and end apart: 4 -> 22, of which waited for: 4 -> 9; matrix products, arithmetic and copies ran while one was open for 6% -> 24% of each run, Pallas kernels for 0% -> 0%
where the time goes in v1:
time: 288 us; the launch traced here: 284 us
  waiting for transfers between devices  109 us (38%)
  matrix products  66.2 us (23%)
  starting transfers between devices  55.9 us (19%)
  blocking collectives  18.5 us (6%)
  other arithmetic  18.4 us (6%)
  local copies, waits for them, and re-layouts  14.4 us (5%)
    dot_general x15, matrix products, matmul(): lax.dot_general(a, b, (((ca,), (cb,)), ((), ())), preferred_element_type=...  66.2 us
    ppermute x6, waiting for transfers between devices, on_device(): code, step = (lax.ppermute(a, 'y', shift('y', k)) for a in (code, step))  30.9 us
    ppermute x3, waiting for transfers between devices, on_device(): lax.ppermute(grad, 'x', shift('x', -j))  29.5 us
    ppermute x3, waiting for transfers between devices, on_device(): lax.ppermute(step, 'x', shift('x', k))  18.9 us
    all_to_all x1, blocking collectives, on_device(): lax.all_to_all(stats, VOCAB, split_axis=0, concat_axis=0, tiled=True)  18.5 us
    all_to_all x2, waiting for transfers between devices, on_device(): lax.all_to_all(a, 'z', split_axis=0, concat_axis=0, tiled=True)  17.8 us
    all_to_all x1, waiting for transfers between devices, on_device(): lax.all_to_all(payload.reshape(vocab_count, capacity, -1), VOCAB, split_a...  11.7 us
    all_to_all x1, starting transfers between devices, on_device(): lax.all_to_all(payload.reshape(vocab_count, capacity, -1), VOCAB, split_a...  11.6 us
  transfers between devices with their start and end apart: 22, of which 9 were waited for; matrix products, arithmetic and copies ran while one was open for 24% of the time, Pallas kernels for 0%

profile of v1, /device:TPU:2, one launch (start us, length us, event | category | flops | bytes accessed | tf_op | source)
XLA Modules:
  0.0 283.9 jit_solution(10734614654850631878)
XLA Ops:
  2.8 3.5 %concatenate.4 = bf16[256,1024]{1,0:T(8,128)(2,1)} concatenate(bf16[192,1024]{1,0:T(8,128)(2,1)S(1)} %copy-done.14, bf16[1,1024]{1,0:T(2,128)(2,1)S(1)} %stack.53, bf16[1,1024]{1,0:T(2,128)(2,1)S(1)} %stack.54, bf16[1,1024]{1,0:T(2,128)(2,1)S(1)} %stack_broadcast_in_dim.3, bf16[61,1024]{1,0:T(8,128)(2,1)S(1)} %broadcast_in_dim.32), dimensions={0} | concatenate | bytes 1048576 | tf_op jit(solution)/shard_map/concatenate | solution.py:65
  6.3 3.8 %fusion.5 = bf16[2048,256]{1,0:T(8,128)(2,1)} fusion(bf16[256,1024]{1,0:T(8,128)(2,1)} %concatenate.4, s32[1024]{0:T(1024)S(1)} %get-tuple-element.21), kind=kOutput, calls=%fused_computation.8 | convolution fusion | flops 1075838976 | bytes 1576960 | tf_op jit(solution)/shard_map/dot_general | solution.py:20
  10.1 11.6 %all-to-all-start = ((bf16[32,64,256]{2,1,0:T(8,128)(2,1)}), bf16[32,64,256]{2,1,0:T(8,128)(2,1)}, u32[]{:S(2)}, u32[]{:S(2)}) async-start(bf16[32,64,256]{2,1,0:T(8,128)(2,1)} %bitcast.140), calls=%async_computation | async-start | bytes 2097152 | tf_op jit(solution)/shard_map/all_to_all | solution.py:67
  21.8 1.3 dynamic-slice_bitcast_fusion
  23.7 5.0 %fusion.38 = f32[192,2048]{1,0:T(8,128)} fusion(bf16[2048,1024]{1,0:T(8,128)(2,1)} %param.5, bf16[4,2,192,1024]{3,2,1,0:T(8,128)(2,1)S(1)} %bitcast.127, s32[]{:T(128)S(6)} %select_n.159, s32[]{:T(128)S(6)} %select_n.149), kind=kOutput, calls=%fused_computation.75 | convolution fusion | flops 805306368 | bytes 6160392 | tf_op jit(solution)/shard_map/dot_general | solution.py:20
  28.7 2.8 fusion.41
  31.5 5.0 %fusion.44 = f32[192,2048]{1,0:T(8,128)} fusion(bf16[2048,1024]{1,0:T(8,128)(2,1)} %param.5, bf16[4,2,192,1024]{3,2,1,0:T(8,128)(2,1)S(1)} %bitcast.129, s32[]{:T(128)S(6)} %select_n.153, s32[]{:T(128)S(6)} %select_n.149), kind=kOutput, calls=%fused_computation.81 | convolution fusion | flops 805306368 | bytes 6160392 | tf_op jit(solution)/shard_map/dot_general | solution.py:20
  36.5 2.7 fusion.47
  39.2 11.7 %all-to-all-done = bf16[32,64,256]{2,1,0:T(8,128)(2,1)} async-done(((bf16[32,64,256]{2,1,0:T(8,128)(2,1)}), bf16[32,64,256]{2,1,0:T(8,128)(2,1)}, u32[]{:S(2)}, u32[]{:S(2)}) %all-to-all-start) | async-done | bytes 1048608 | tf_op jit(solution)/shard_map/all_to_all | solution.py:67
  50.9 1.3 slice_convert_fusion
  53.6 3.9 %abs_reduce_fusion.3 = (f32[192]{0:T(256)S(1)}, f32[192,2048]{1,0:T(8,128)S(1)}) fusion(f32[192,2048]{1,0:T(8,128)S(1)} %copy-done.10, bf16[2048,1024]{1,0:T(8,128)(2,1)} %collective-permute-done.1, bf16[4,192,1024]{2,1,0:T(8,128)(2,1)} %collective-permute-done, s32[]{:T(128)S(6)} %select_n.152), kind=kOutput, calls=%fused_computation.62 | convolution fusion | flops 806485824 | bytes 7734020 | tf_op jit(solution)/shard_map/dot_general | solution.py:20
  57.6 4.1 %abs_reduce_fusion.2 = (f32[192]{0:T(256)S(1)}, f32[192,2048]{1,0:T(8,128)S(1)}) fusion(f32[192,2048]{1,0:T(8,128)S(1)} %copy-done.9, bf16[2048,1024]{1,0:T(8,128)(2,1)} %collective-permute-done.1, bf16[4,192,1024]{2,1,0:T(8,128)(2,1)} %collective-permute-done, s32[]{:T(128)S(6)} %select_n.155), kind=kOutput, calls=%fused_computation.60 | convolution fusion | flops 806485824 | bytes 7734020 | tf_op jit(solution)/shard_map/dot_general | solution.py:20
  61.7 4.0 %abs_reduce_fusion.1 = (f32[192]{0:T(256)S(1)}, f32[192,2048]{1,0:T(8,128)S(1)}) fusion(f32[192,2048]{1,0:T(8,128)S(1)} %copy-done.8, bf16[2048,1024]{1,0:T(8,128)(2,1)} %collective-permute-done.1, bf16[4,192,1024]{2,1,0:T(8,128)(2,1)} %collective-permute-done, s32[]{:T(128)S(6)} %select_n.158), kind=kOutput, calls=%fused_computation.58 | convolution fusion | flops 806485824 | bytes 7734020 | tf_op jit(solution)/shard_map/dot_general | solution.py:20
  66.9 1.6 collective-permute-start.4
  68.7 3.6 %collective-permute-start.2 = (s16[192,2048]{1,0:T(8,128)(2,1)S(1)}, s16[192,2048]{1,0:T(8,128)(2,1)S(1)}, u32[]{:S(2)}, u32[]{:S(2)}) collective-permute-start(s16[192,2048]{1,0:T(8,128)(2,1)S(1)} %round-nearest-even_convert_fusion.3), channel_id=1, source_target_pairs={{0,128},{64,192},{128,0},{192,64},{1,129},{65,193},{129,1},{193,65... | collective-permute-start | bytes 2359304 | tf_op jit(solution)/shard_map/ppermute | solution.py:87
  72.3 4.9 %fusion = f32[256,2048]{1,0:T(8,128)S(1)} fusion(bf16[2048,256]{1,0:T(8,128)(2,1)} %bitcast.1, s32[2048]{0:T(1024)S(1)} %fusion.35), kind=kOutput, calls=%fused_computation.1 | convolution fusion | flops 2151677952 | bytes 3153920 | tf_op jit(solution)/shard_map/dot_general | solution.py:20
  77.7 1.9 collective-permute-start.5
  79.6 17.4 %collective-permute-done.7 = f32[192,1]{0,1:T(1,128)S(1)} collective-permute-done((f32[192,1]{0,1:T(1,128)S(1)}, f32[192,1]{0,1:T(1,128)S(1)}, u32[]{:S(2)}, u32[]{:S(2)}) %collective-permute-start.7) | collective-permute-done | bytes 800 | tf_op jit(solution)/shard_map/ppermute | solution.py:87
  96.9 5.2 %collective-permute-start.3 = (f32[192,1]{0,1:T(1,128)S(1)}, f32[192,1]{0,1:T(1,128)S(1)}, u32[]{:S(2)}, u32[]{:S(2)}) collective-permute-start(f32[192,1]{0,1:T(1,128)S(1)} %bitcast.146), channel_id=1, source_target_pairs={{0,128},{64,192},{128,0},{192,64},{1,129},{65,193},{129,1},{193,65... | collective-permute-start | bytes 2312 | tf_op jit(solution)/shard_map/ppermute | solution.py:87
  102.2 1.5 collective-permute-done.3
  103.7 4.7 %select_reduce_fusion.1 = (f32[192]{0:T(256)S(1)}, f32[192,2048]{1,0:T(8,128)S(1)}) fusion(pred[2048]{0:T(1024)(128)(4,1)S(1)} %compare_reduce_fusion, f32[192]{0:T(256)S(1)} %bitcast.149, s16[192,2048]{1,0:T(8,128)(2,1)S(1)} %collective-permute-done.6, f32[192]{0:T(256)S(1)} %bitcast.150, s16[192,2048]{1,0:T(8,128)(2,1)S(1)} %collective-permute-done.4, ...), kind=kOutput, calls=%fused_computation.56 | convolution fusion | flops 810024768 | bytes 10097668 | tf_op jit(solution)/shard_map/dot_general | solution.py:20
  108.8 18.5 %all_to_all.25 = f32[32,3,192]{2,1,0:T(4,128)S(1)} all-to-all(f32[32,3,192]{2,1,0:T(4,128)S(1)} %broadcast_in_dim.63), channel_id=1, replica_groups=mesh['x'=4,'core'=2,'y'=4,'z'=8] {'y','z'}, dimensions={0} | all-to-all | bytes 147456 | tf_op jit(solution)/shard_map/all_to_all | solution.py:98
  128.1 1.7 collective-permute-start.10
  129.8 2.0 collective-permute-start.9
  131.8 2.5 collective-permute-start.8
  134.4 14.3 %collective-permute-done.10 = bf16[192,2048]{1,0:T(8,128)(2,1)S(1)} collective-permute-done((bf16[192,2048]{1,0:T(8,128)(2,1)S(1)}, bf16[192,2048]{1,0:T(8,128)(2,1)S(1)}, u32[]{:S(2)}, u32[]{:S(2)}) %collective-permute-start.10) | collective-permute-done | bytes 786464 | tf_op jit(solution)/shard_map/ppermute | solution.py:105
  148.7 3.1 %collective-permute-done.9 = bf16[192,2048]{1,0:T(8,128)(2,1)S(1)} collective-permute-done((bf16[192,2048]{1,0:T(8,128)(2,1)S(1)}, bf16[192,2048]{1,0:T(8,128)(2,1)S(1)}, u32[]{:S(2)}, u32[]{:S(2)}) %collective-permute-start.9) | collective-permute-done | bytes 786464 | tf_op jit(solution)/shard_map/ppermute | solution.py:105
  151.8 12.0 %collective-permute-done.8 = bf16[192,2048]{1,0:T(8,128)(2,1)S(1)} collective-permute-done((bf16[192,2048]{1,0:T(8,128)(2,1)S(1)}, bf16[192,2048]{1,0:T(8,128)(2,1)S(1)}, u32[]{:S(2)}, u32[]{:S(2)}) %collective-permute-start.8) | collective-permute-done | bytes 786464 | tf_op jit(solution)/shard_map/ppermute | solution.py:105
  163.9 1.9 pad_maximum_fusion.1
  166.1 3.9 %fusion.1 = bf16[2048,192]{1,0:T(8,128)(2,1)} fusion(s32[2048]{0:T(1024)S(1)} %fusion.35, f32[192,2048]{1,0:T(8,128)S(1)} %get-tuple-element.45), kind=kOutput, calls=%fused_computation.2 | convolution fusion | flops 1615200256 | bytes 2367488 | tf_op jit(solution)/shard_map/dot_general | solution.py:20
  170.0 4.8 %all-to-all-start.1 = ((bf16[32,64,192]{2,1,0:T(8,128)(2,1)}), bf16[32,64,192]{2,1,0:T(8,128)(2,1)}, u32[]{:S(2)}, u32[]{:S(2)}) async-start(bf16[32,64,192]{2,1,0:T(8,128)(2,1)} %bitcast.141), calls=%async_computation.1 | async-start | bytes 2097152 | tf_op jit(solution)/shard_map/all_to_all | solution.py:129
  174.8 2.2 select_bitcast_fusion.1
  178.7 2.1 copy-done
  182.1 6.9 %fusion.6 = f32[4,384,1024]{2,1,0:T(8,128)S(1)} fusion(bf16[4,384,2048]{2,1,0:T(8,128)(2,1)S(1)} %bitcast.132, bf16[2048,1024]{1,0:T(8,128)(2,1)S(1)} %copy-done.17), kind=kOutput, calls=%fused_computation.10 | convolution fusion | flops 6442450944 | bytes 16777216 | tf_op jit(solution)/shard_map/dot_general | solution.py:20
  189.4 1.8 fusion.29
  191.2 1.4 copy-done.1
  192.6 3.2 %collective-permute-start.12 = (s16[384,1024]{1,0:T(8,128)(2,1)}, s16[384,1024]{1,0:T(8,128)(2,1)S(1)}, u32[]{:S(2)}, u32[]{:S(2)}) collective-permute-start(s16[384,1024]{1,0:T(8,128)(2,1)} %get-tuple-element.10), channel_id=1, source_target_pairs={{0,16},{8,24},{16,0},{24,8},{1,17},{9,25},{17,1},{25,9},{2,18},{10... | collective-permute-start | bytes 2359304 | tf_op jit(solution)/shard_map/ppermute | solution.py:119
  198.7 1.6 constant_dynamic-slice_fusion.3
  200.3 2.6 collective-permute-start.17
  203.0 30.9 %collective-permute-done.15 = f32[384,1]{0,1:T(1,128)S(1)} collective-permute-done((f32[384,1]{0,1:T(1,128)S(1)}, f32[384,1]{0,1:T(1,128)S(1)}, u32[]{:S(2)}, u32[]{:S(2)}) %collective-permute-start.15) | collective-permute-done | bytes 1568 | tf_op jit(solution)/shard_map/ppermute | solution.py:119
  233.9 1.6 collective-permute-start.13
  235.5 3.7 %fusion.4 = bf16[192,1024]{1,0:T(8,128)(2,1)} fusion(bf16[2048,192]{1,0:T(8,128)(2,1)} %bitcast.19, s32[1024]{0:T(1024)S(1)} %get-tuple-element.21), kind=kOutput, calls=%fused_computation.7 | convolution fusion | flops 807403520 | bytes 1183744 | tf_op jit(solution)/shard_map/dot_general | solution.py:20
  240.1 3.3 %abs_reduce_fusion = (f32[384]{0:T(512)S(1)}, f32[384,1024]{1,0:T(8,128)S(1)}) fusion(f32[384]{0:T(512)S(1)} %reduce.7, s16[384,1024]{1,0:T(8,128)(2,1)} %collective-permute-done.16, f32[384]{0:T(512)S(1)} %reduce.6, s16[384,1024]{1,0:T(8,128)(2,1)} %collective-permute-done.14, f32[384]{0:T(512)S(1)} %reduce.5, s16[384,1024]{1,0:T(8,128)(2,1)} %copy-done.13, ...), kind=kLoop, calls=%fused_computation.53 | loop fusion | flops 4324992 | bytes 5511172 | tf_op jit(solution)/shard_map/reduce_max | solution.py:28
  244.2 5.4 %all-to-all-start.4 = ((f32[8,48,1]{1,2,0:T(1,128)}), f32[8,48,1]{1,2,0:T(1,128)S(1)}, u32[]{:S(2)}, u32[]{:S(2)}) async-start(f32[8,48,1]{1,2,0:T(1,128)} %mul.313), calls=%async_computation.4 | async-start | bytes 8192 | tf_op jit(solution)/shard_map/all_to_all | solution.py:124
  250.7 6.4 %all-to-all-done.4 = f32[8,48,1]{1,2,0:T(1,128)S(1)} async-done(((f32[8,48,1]{1,2,0:T(1,128)}), f32[8,48,1]{1,2,0:T(1,128)S(1)}, u32[]{:S(2)}, u32[]{:S(2)}) %all-to-all-start.4) | async-done | bytes 1568 | tf_op jit(solution)/shard_map/all_to_all | solution.py:124
  257.2 3.5 %all-to-all-start.3 = ((s16[8,48,1024]{2,1,0:T(8,128)(2,1)}), s16[8,48,1024]{2,1,0:T(8,128)(2,1)S(1)}, u32[]{:S(2)}, u32[]{:S(2)}) async-start(s16[8,48,1024]{2,1,0:T(8,128)(2,1)} %round-nearest-even_convert_fusion), calls=%async_computation.3 | async-start | bytes 1572864 | tf_op jit(solution)/shard_map/all_to_all | solution.py:124
  260.7 10.4 %bitcast_convert_fusion = bf16[2048,1024]{1,0:T(8,128)(2,1)} fusion(bf16[1,2,192,1024]{3,2,1,0:T(8,128)(2,1)S(1)} %get-tuple-element.16, bf16[1,2,192,1024]{3,2,1,0:T(8,128)(2,1)S(1)} %copy-done.12, bf16[1,2,192,1024]{3,2,1,0:T(8,128)(2,1)} %get-tuple-element.18, bf16[1,2,192,1024]{3,2,1,0:T(8,128)(2,1)S(1)} %get-tuple-element.15, ...), kind=kOutput, calls=%fused_computation.3 | convolution fusion | flops 6449266688 | bytes 13631488 | tf_op jit(solution)/shard_map/dot_general | solution.py:20
  271.1 11.4 %all-to-all-done.3 = s16[8,48,1024]{2,1,0:T(8,128)(2,1)S(1)} async-done(((s16[8,48,1024]{2,1,0:T(8,128)(2,1)}), s16[8,48,1024]{2,1,0:T(8,128)(2,1)S(1)}, u32[]{:S(2)}, u32[]{:S(2)}) %all-to-all-start.3) | async-done | bytes 786464 | tf_op jit(solution)/shard_map/all_to_all | solution.py:124
  (93 shorter events, 17.8 us)
Async XLA Ops:
  0.6 2.2 copy-start.14
  0.6 52.5 %collective-permute-start.1 = (bf16[2048,1024]{1,0:T(8,128)(2,1)}, bf16[2048,1024]{1,0:T(8,128)(2,1)}, u32[]{:S(2)}, u32[]{:S(2)}) collective-permute-start(bf16[2048,1024]{1,0:T(8,128)(2,1)} %param.5), channel_id=1, source_target_pairs={{0,32},{32,0},{1,33},{33,1},{2,34},{34,2},{3,35},{35,3},{4,36},{36... | collective-permute-start | bytes 12582920 | tf_op jit(solution)/shard_map/ppermute | solution.py:55
  6.3 15.5 %copy-start.2 = (bf16[1536,1024]{1,0:T(8,128)(2,1)S(1)}, bf16[1536,1024]{1,0:T(8,128)(2,1)}, u32[]{:S(2)}) copy-start(bf16[1536,1024]{1,0:T(8,128)(2,1)} %param.4) | copy-start | bytes 9437188
  10.1 40.8 %all-to-all-start = ((bf16[32,64,256]{2,1,0:T(8,128)(2,1)}), bf16[32,64,256]{2,1,0:T(8,128)(2,1)}, u32[]{:S(2)}, u32[]{:S(2)}) async-start(bf16[32,64,256]{2,1,0:T(8,128)(2,1)} %bitcast.140), calls=%async_computation | async-start | bytes 2097152 | tf_op jit(solution)/shard_map/all_to_all | solution.py:67
  23.1 30.0 %collective-permute-start = (bf16[4,192,1024]{2,1,0:T(8,128)(2,1)}, bf16[4,192,1024]{2,1,0:T(8,128)(2,1)}, u32[]{:S(2)}, u32[]{:S(2)}) collective-permute-start(bf16[4,192,1024]{2,1,0:T(8,128)(2,1)} %dynamic-slice_bitcast_fusion), channel_id=1, source_target_pairs={{0,32},{32,0},{1,33},{33,1},{2,34},{34,2},{3,35},{35,3},{4,36},{36... | collective-permute-start | bytes 4718600 | tf_op jit(solution)/shard_map/ppermute | solution.py:57
  23.7 5.0 %copy-start.15 = (bf16[2048,1024]{1,0:T(8,128)(2,1)S(1)}, bf16[2048,1024]{1,0:T(8,128)(2,1)}, u32[]{:S(2)}) copy-start(bf16[2048,1024]{1,0:T(8,128)(2,1)} %param.5) | copy-start | bytes 12582916
  31.5 5.0 %copy-start.16 = (bf16[2048,1024]{1,0:T(8,128)(2,1)S(1)}, bf16[2048,1024]{1,0:T(8,128)(2,1)}, u32[]{:S(2)}) copy-start(bf16[2048,1024]{1,0:T(8,128)(2,1)} %param.5) | copy-start | bytes 12582916
  52.2 1.4 copy-start.10
  53.1 4.5 %copy-start.9 = (f32[192,2048]{1,0:T(8,128)S(1)}, f32[192,2048]{1,0:T(8,128)}, u32[]{:S(2)}) copy-start(f32[192,2048]{1,0:T(8,128)} %fusion.41) | copy-start | bytes 4718596
  57.6 4.1 %copy-start.8 = (f32[192,2048]{1,0:T(8,128)S(1)}, f32[192,2048]{1,0:T(8,128)}, u32[]{:S(2)}) copy-start(f32[192,2048]{1,0:T(8,128)} %fusion.38) | copy-start | bytes 4718596
  65.9 37.8 %collective-permute-start.6 = (s16[192,2048]{1,0:T(8,128)(2,1)S(1)}, s16[192,2048]{1,0:T(8,128)(2,1)S(1)}, u32[]{:S(2)}, u32[]{:S(2)}) collective-permute-start(s16[192,2048]{1,0:T(8,128)(2,1)S(1)} %round-nearest-even_convert_fusion.1), channel_id=1, source_target_pairs={{0,192},{64,0},{128,64},{192,128},{1,193},{65,1},{129,65},{193,129... | collective-permute-start | bytes 2359304 | tf_op jit(solution)/shard_map/ppermute | solution.py:87
  66.9 36.8 %collective-permute-start.4 = (s16[192,2048]{1,0:T(8,128)(2,1)S(1)}, s16[192,2048]{1,0:T(8,128)(2,1)S(1)}, u32[]{:S(2)}, u32[]{:S(2)}) collective-permute-start(s16[192,2048]{1,0:T(8,128)(2,1)S(1)} %round-nearest-even_convert_fusion.2), channel_id=1, source_target_pairs={{0,64},{64,128},{128,192},{192,0},{1,65},{65,129},{129,193},{193,1... | collective-permute-start | bytes 2359304 | tf_op jit(solution)/shard_map/ppermute | solution.py:87
  68.7 35.0 %collective-permute-start.2 = (s16[192,2048]{1,0:T(8,128)(2,1)S(1)}, s16[192,2048]{1,0:T(8,128)(2,1)S(1)}, u32[]{:S(2)}, u32[]{:S(2)}) collective-permute-start(s16[192,2048]{1,0:T(8,128)(2,1)S(1)} %round-nearest-even_convert_fusion.3), channel_id=1, source_target_pairs={{0,128},{64,192},{128,0},{192,64},{1,129},{65,193},{129,1},{193,65... | collective-permute-start | bytes 2359304 | tf_op jit(solution)/shard_map/ppermute | solution.py:87
  77.2 26.5 %copy-start.11 = (f32[192,2048]{1,0:T(8,128)S(1)}, f32[192,2048]{1,0:T(8,128)}, u32[]{:S(2)}) copy-start(f32[192,2048]{1,0:T(8,128)} %fusion.47) | copy-start | bytes 4718596
  77.2 19.7 %collective-permute-start.7 = (f32[192,1]{0,1:T(1,128)S(1)}, f32[192,1]{0,1:T(1,128)S(1)}, u32[]{:S(2)}, u32[]{:S(2)}) collective-permute-start(f32[192,1]{0,1:T(1,128)S(1)} %bitcast.148), channel_id=1, source_target_pairs={{0,192},{64,0},{128,64},{192,128},{1,193},{65,1},{129,65},{193,129... | collective-permute-start | bytes 2312 | tf_op jit(solution)/shard_map/ppermute | solution.py:87
  77.7 24.5 %collective-permute-start.5 = (f32[192,1]{0,1:T(1,128)S(1)}, f32[192,1]{0,1:T(1,128)S(1)}, u32[]{:S(2)}, u32[]{:S(2)}) collective-permute-start(f32[192,1]{0,1:T(1,128)S(1)} %bitcast.147), channel_id=1, source_target_pairs={{0,64},{64,128},{128,192},{192,0},{1,65},{65,129},{129,193},{193,1... | collective-permute-start | bytes 2312 | tf_op jit(solution)/shard_map/ppermute | solution.py:87
  96.9 6.8 %collective-permute-start.3 = (f32[192,1]{0,1:T(1,128)S(1)}, f32[192,1]{0,1:T(1,128)S(1)}, u32[]{:S(2)}, u32[]{:S(2)}) collective-permute-start(f32[192,1]{0,1:T(1,128)S(1)} %bitcast.146), channel_id=1, source_target_pairs={{0,128},{64,192},{128,0},{192,64},{1,129},{65,193},{129,1},{193,65... | collective-permute-start | bytes 2312 | tf_op jit(solution)/shard_map/ppermute | solution.py:87
  128.1 20.6 %collective-permute-start.10 = (bf16[192,2048]{1,0:T(8,128)(2,1)S(1)}, bf16[192,2048]{1,0:T(8,128)(2,1)S(1)}, u32[]{:S(2)}, u32[]{:S(2)}) collective-permute-start(bf16[192,2048]{1,0:T(8,128)(2,1)S(1)} %select_convert_fusion), channel_id=1, source_target_pairs={{0,64},{64,128},{128,192},{192,0},{1,65},{65,129},{129,193},{193,1... | collective-permute-start | bytes 2359304 | tf_op jit(solution)/shard_map/ppermute | solution.py:105
  129.8 22.0 %collective-permute-start.9 = (bf16[192,2048]{1,0:T(8,128)(2,1)S(1)}, bf16[192,2048]{1,0:T(8,128)(2,1)S(1)}, u32[]{:S(2)}, u32[]{:S(2)}) collective-permute-start(bf16[192,2048]{1,0:T(8,128)(2,1)S(1)} %select_convert_fusion), channel_id=1, source_target_pairs={{0,128},{64,192},{128,0},{192,64},{1,129},{65,193},{129,1},{193,65... | collective-permute-start | bytes 2359304 | tf_op jit(solution)/shard_map/ppermute | solution.py:105
  131.8 32.0 %collective-permute-start.8 = (bf16[192,2048]{1,0:T(8,128)(2,1)S(1)}, bf16[192,2048]{1,0:T(8,128)(2,1)S(1)}, u32[]{:S(2)}, u32[]{:S(2)}) collective-permute-start(bf16[192,2048]{1,0:T(8,128)(2,1)S(1)} %select_convert_fusion), channel_id=1, source_target_pairs={{0,192},{64,0},{128,64},{192,128},{1,193},{65,1},{129,65},{193,129... | collective-permute-start | bytes 2359304 | tf_op jit(solution)/shard_map/ppermute | solution.py:105
  151.8 14.0 %copy-start.4 = (bf16[192,2048]{1,0:T(8,128)(2,1)}, bf16[192,2048]{1,0:T(8,128)(2,1)S(1)}, u32[]{:S(2)}) copy-start(bf16[192,2048]{1,0:T(8,128)(2,1)S(1)} %collective-permute-done.9) | copy-start | bytes 2359300
  163.9 1.9 copy-start.6
  165.8 9.0 %collective-permute-start.11 = (bf16[4,192,2048]{2,1,0:T(8,128)(2,1)}, bf16[4,192,2048]{2,1,0:T(8,128)(2,1)}, u32[]{:S(2)}, u32[]{:S(2)}) collective-permute-start(bf16[4,192,2048]{2,1,0:T(8,128)(2,1)} %pad_maximum_fusion.1), channel_id=1, source_target_pairs={{0,32},{32,0},{1,33},{33,1},{2,34},{34,2},{3,35},{35,3},{4,36},{36... | collective-permute-start | bytes 9437192 | tf_op jit(solution)/shard_map/ppermute | solution.py:107
  169.9 4.8 %copy-start.5 = (bf16[192,2048]{1,0:T(8,128)(2,1)S(1)}, bf16[192,2048]{1,0:T(8,128)(2,1)}, u32[]{:S(2)}) copy-start(bf16[192,2048]{1,0:T(8,128)(2,1)} %copy-done.4) | copy-start | bytes 2359300
  169.9 4.8 %copy-start.7 = (bf16[192,2048]{1,0:T(8,128)(2,1)S(1)}, bf16[192,2048]{1,0:T(8,128)(2,1)}, u32[]{:S(2)}) copy-start(bf16[192,2048]{1,0:T(8,128)(2,1)} %copy-done.6) | copy-start | bytes 2359300
  170.0 65.5 %all-to-all-start.1 = ((bf16[32,64,192]{2,1,0:T(8,128)(2,1)}), bf16[32,64,192]{2,1,0:T(8,128)(2,1)}, u32[]{:S(2)}, u32[]{:S(2)}) async-start(bf16[32,64,192]{2,1,0:T(8,128)(2,1)} %bitcast.141), calls=%async_computation.1 | async-start | bytes 2097152 | tf_op jit(solution)/shard_map/all_to_all | solution.py:129
  177.6 3.2 %copy-start = (bf16[4,2,192,2048]{3,2,0,1:T(8,128)(2,1)}, bf16[4,2,192,2048]{3,2,0,1:T(8,128)(2,1)S(1)}, u32[]{:S(2)}) copy-start(bf16[4,2,192,2048]{3,2,0,1:T(8,128)(2,1)S(1)} %pad_maximum_fusion) | copy-start | bytes 18874372
  177.6 4.5 %copy-start.17 = (bf16[2048,1024]{1,0:T(8,128)(2,1)S(1)}, bf16[2048,1024]{1,0:T(8,128)(2,1)}, u32[]{:S(2)}) copy-start(bf16[2048,1024]{1,0:T(8,128)(2,1)} %param.5) | copy-start | bytes 12582916
  188.9 3.7 %copy-start.1 = (f32[4,384,1024]{2,1,0:T(8,128)}, f32[4,384,1024]{2,1,0:T(8,128)S(1)}, u32[]{:S(2)}) copy-start(f32[4,384,1024]{2,1,0:T(8,128)S(1)} %fusion.6) | copy-start | bytes 18874372
  189.4 9.3 %copy-start.3 = (bf16[1536,1024]{1,0:T(8,128)(2,1)S(1)}, bf16[1536,1024]{1,0:T(8,128)(2,1)}, u32[]{:S(2)}) copy-start(bf16[1536,1024]{1,0:T(8,128)(2,1)} %param.4) | copy-start | bytes 9437188
  192.6 46.6 %collective-permute-start.12 = (s16[384,1024]{1,0:T(8,128)(2,1)}, s16[384,1024]{1,0:T(8,128)(2,1)S(1)}, u32[]{:S(2)}, u32[]{:S(2)}) collective-permute-start(s16[384,1024]{1,0:T(8,128)(2,1)} %get-tuple-element.10), channel_id=1, source_target_pairs={{0,16},{8,24},{16,0},{24,8},{1,17},{9,25},{17,1},{25,9},{2,18},{10... | collective-permute-start | bytes 2359304 | tf_op jit(solution)/shard_map/ppermute | solution.py:119
  195.8 43.4 %collective-permute-start.16 = (s16[384,1024]{1,0:T(8,128)(2,1)}, s16[384,1024]{1,0:T(8,128)(2,1)}, u32[]{:S(2)}, u32[]{:S(2)}) collective-permute-start(s16[384,1024]{1,0:T(8,128)(2,1)} %get-tuple-element.11), channel_id=1, source_target_pairs={{0,24},{8,0},{16,8},{24,16},{1,25},{9,1},{17,9},{25,17},{2,26},{10... | collective-permute-start | bytes 2359304 | tf_op jit(solution)/shard_map/ppermute | solution.py:119
  197.0 43.2 %collective-permute-start.14 = (s16[384,1024]{1,0:T(8,128)(2,1)S(1)}, s16[384,1024]{1,0:T(8,128)(2,1)}, u32[]{:S(2)}, u32[]{:S(2)}) collective-permute-start(s16[384,1024]{1,0:T(8,128)(2,1)S(1)} %get-tuple-element.12), channel_id=1, source_target_pairs={{0,8},{8,16},{16,24},{24,0},{1,9},{9,17},{17,25},{25,1},{2,10},{10... | collective-permute-start | bytes 2359304 | tf_op jit(solution)/shard_map/ppermute | solution.py:119
  198.1 35.8 %collective-permute-start.15 = (f32[384,1]{0,1:T(1,128)S(1)}, f32[384,1]{0,1:T(1,128)S(1)}, u32[]{:S(2)}, u32[]{:S(2)}) collective-permute-start(f32[384,1]{0,1:T(1,128)S(1)} %mul.299), channel_id=1, source_target_pairs={{0,8},{8,16},{16,24},{24,0},{1,9},{9,17},{17,25},{25,1},{2,10},{10... | collective-permute-start | bytes 4616 | tf_op jit(solution)/shard_map/ppermute | solution.py:119
  200.3 38.9 %collective-permute-start.17 = (f32[384,1]{0,1:T(1,128)S(1)}, f32[384,1]{0,1:T(1,128)S(1)}, u32[]{:S(2)}, u32[]{:S(2)}) collective-permute-start(f32[384,1]{0,1:T(1,128)S(1)} %mul.306), channel_id=1, source_target_pairs={{0,24},{8,0},{16,8},{24,16},{1,25},{9,1},{17,9},{25,17},{2,26},{10... | collective-permute-start | bytes 4616 | tf_op jit(solution)/shard_map/ppermute | solution.py:119
  233.9 5.3 %collective-permute-start.13 = (f32[384,1]{0,1:T(1,128)S(1)}, f32[384,1]{0,1:T(1,128)S(1)}, u32[]{:S(2)}, u32[]{:S(2)}) collective-permute-start(f32[384,1]{0,1:T(1,128)S(1)} %mul.292), channel_id=1, source_target_pairs={{0,16},{8,24},{16,0},{24,8},{1,17},{9,25},{17,1},{25,9},{2,18},{10... | collective-permute-start | bytes 4616 | tf_op jit(solution)/shard_map/ppermute | solution.py:119
  239.3 0.9 copy-start.13
  244.2 13.0 %all-to-all-start.4 = ((f32[8,48,1]{1,2,0:T(1,128)}), f32[8,48,1]{1,2,0:T(1,128)S(1)}, u32[]{:S(2)}, u32[]{:S(2)}) async-start(f32[8,48,1]{1,2,0:T(1,128)} %mul.313), calls=%async_computation.4 | async-start | bytes 8192 | tf_op jit(solution)/shard_map/all_to_all | solution.py:124
  250.7 10.0 %copy-start.12 = (bf16[1,2,192,1024]{3,2,1,0:T(8,128)(2,1)S(1)}, bf16[1,2,192,1024]{3,2,1,0:T(8,128)(2,1)}, u32[]{:S(2)}) copy-start(bf16[1,2,192,1024]{3,2,1,0:T(8,128)(2,1)} %get-tuple-element.17) | copy-start | bytes 2359300
  257.2 25.3 %all-to-all-start.3 = ((s16[8,48,1024]{2,1,0:T(8,128)(2,1)}), s16[8,48,1024]{2,1,0:T(8,128)(2,1)S(1)}, u32[]{:S(2)}, u32[]{:S(2)}) async-start(s16[8,48,1024]{2,1,0:T(8,128)(2,1)} %round-nearest-even_convert_fusion), calls=%async_computation.3 | async-start | bytes 1572864 | tf_op jit(solution)/shard_map/all_to_all | solution.py:124
